TPU v7x, 256 devices: a whole 4x4x8 slice. The times are simulated.
256 devices in a mesh: pool: 4 (over y), ep: 64 (over z, x, core).
Axes of the slice: x: 4, y: 4, z: 8, core: 2. Of those that a mesh axis runs over, the one named last changes fastest.
Arguments:
- residual: bfloat16 [2048, 4096], P(('pool', 'ep')), may hold values from -6 to 6
- queries: bfloat16 [2048, 8192], P(('pool', 'ep')), may hold values from -6 to 6
- token_keys: bfloat16 [2048, 512], P(('pool', 'ep')), may hold values from -6 to 6
- token_values: bfloat16 [2048, 512], P(('pool', 'ep')), may hold values from -6 to 6
- resident_cache: bfloat16 [2048, 2, 64, 512], P(('pool', 'ep')), may hold values from -6 to 6
- pool_block_cache: bfloat16 [64, 128, 2, 16, 512], P('ep', 'pool'), may hold values from -6 to 6
- block_table: int32 [2048, 4], P(('pool', 'ep')), may hold values from 0 to 127, as said below
- resumed: int32 [2048], P(('pool', 'ep')), may hold values from 0 to 1, as said below
- lengths: int32 [2048], P(('pool', 'ep')), may hold values from 2 to 64
- out_proj: bfloat16 [8192, 4096], P('ep'), may hold values from -0.0625 to 0.0625
- norm_gain: bfloat16 [4096], replicated, may hold values from 0.25 to 1.75
- expert_ids: int32 [2048, 8], P(('pool', 'ep')), may hold values from 0 to 63, all different within a row; in each aligned block of 8 rows (0 to 7, 8 to 15, ...) at most 2 rows name the same one
- route_scores: float32 [2048, 8], P(('pool', 'ep')), may hold values from 0.05 to 1
- expert_gate: bfloat16 [64, 4096, 1536], P('ep', None, 'pool'), may hold values from -0.09375 to 0.09375
- expert_up: bfloat16 [64, 4096, 1536], P('ep', None, 'pool'), may hold values from -0.09375 to 0.09375
- expert_down: bfloat16 [64, 1536, 4096], P('ep', 'pool'), may hold values from -0.15625 to 0.15625
Outputs:
- attended: bfloat16 [2048, 4096], P(('pool', 'ep'))
- layer_out: bfloat16 [2048, 4096], P(('pool', 'ep'))
Inputs may be any that keep to these rules, and one draw needn't show every extreme that they name: `block_table`: entry // 32 is the pool index that holds the block, within the pool of the row's ep index; every row has 1 of its blocks on each pool index. At most 4 rows of one device are resumed; the first device has exactly 4. `expert_ids`: among the rows of one device no expert is named more than 2 times, a bound that some block reaches.
All inputs are finite; a program needn't handle non-finite values.
Results may differ from a plain program's by a relative error of at most 0.012.
Values may be sent and summed in bfloat16 or wider, within the bound.
No kernel may reach another device: no remote copies, remote signals or barrier semaphores. Data moves between devices by JAX's collectives and lax.ppermute only.
A program may use at most 128 MiB of HBM per device.

v0:
```python
import math

import jax
import jax.numpy as jnp
from jax import lax
from jax.sharding import PartitionSpec as P

D = 4096
QUERY_HEADS = 64
KEY_VALUE_HEADS = 4
HEAD_SIZE = 128
CONTEXT_LIMIT = 64
BLOCK_POSITIONS = 16


NEG_FILL = -1e30
NORM_EPSILON = 1e-06


def attend_rows(queries, active_cache, token_keys, token_values, lengths):
    total_rows = queries.shape[0]
    group_query_heads = QUERY_HEADS // KEY_VALUE_HEADS
    query_matrix = queries.reshape(total_rows, KEY_VALUE_HEADS, group_query_heads, HEAD_SIZE)
    key_portion = active_cache[:, 0].reshape(total_rows, CONTEXT_LIMIT, KEY_VALUE_HEADS, HEAD_SIZE)
    value_portion = active_cache[:, 1].reshape(
        total_rows, CONTEXT_LIMIT, KEY_VALUE_HEADS, HEAD_SIZE
    )
    self_key = token_keys.reshape(total_rows, KEY_VALUE_HEADS, HEAD_SIZE)
    self_value = token_values.reshape(total_rows, KEY_VALUE_HEADS, HEAD_SIZE)
    factor = 1.0 / math.sqrt(HEAD_SIZE)
    scores = (
        jnp.einsum("rkgd,rtkd->rkgt", query_matrix, key_portion, preferred_element_type=jnp.float32)
        * factor
    )
    own_score = (
        jnp.einsum("rkgd,rkd->rkg", query_matrix, self_key, preferred_element_type=jnp.float32)
        * factor
    )
    live_mask = (jnp.arange(CONTEXT_LIMIT)[None, :] < lengths[:, None])[:, None, None, :]
    scores = jnp.where(live_mask, scores, NEG_FILL)
    highest = jnp.maximum(jnp.max(scores, axis=-1), own_score)
    raised = jnp.where(live_mask, jnp.exp(scores - highest[..., None]), 0.0)
    own_raised = jnp.exp(own_score - highest)
    denominator = jnp.sum(raised, axis=-1) + own_raised
    weights = (raised / denominator[..., None]).astype(jnp.bfloat16)
    own_weight = (own_raised / denominator).astype(jnp.bfloat16)
    context = jnp.einsum(
        "rkgt,rtkd->rkgd", weights, value_portion, preferred_element_type=jnp.float32
    )
    context = (
        context
        + own_weight.astype(jnp.float32)[..., None] * self_value.astype(jnp.float32)[:, :, None, :]
    )
    return context.reshape(total_rows, QUERY_HEADS * HEAD_SIZE).astype(jnp.bfloat16)


def shards(
    residual,
    queries,
    token_keys,
    token_values,
    resident_cache,
    pool_block_cache,
    block_table,
    resumed,
    lengths,
    out_proj,
    norm_gain,
    expert_ids,
    route_scores,
    expert_gate,
    expert_up,
    expert_down,
):
    total_rows = residual.shape[0]
    expert_count = lax.axis_size("ep")
    row_block_count = block_table.shape[1]
    block_layout = (total_rows, row_block_count, 2, BLOCK_POSITIONS, KEY_VALUE_HEADS * HEAD_SIZE)
    empty_blocks = jnp.zeros(block_layout, jnp.bfloat16)
    shard_piece = lax.all_gather(pool_block_cache, "pool", axis=1, tiled=True)
    piece_rows = shard_piece.shape[1]
    inside = (block_table >= 0) & (block_table < piece_rows)
    chosen = jnp.take(shard_piece[0], jnp.clip(block_table, 0, piece_rows - 1), axis=0)
    loaded_cache = jnp.where(inside[:, :, None, None, None], chosen, empty_blocks)
    ordered_blocks = jnp.transpose(loaded_cache, (0, 2, 1, 3, 4)).reshape(
        total_rows, 2, CONTEXT_LIMIT, KEY_VALUE_HEADS * HEAD_SIZE
    )
    active_cache = jnp.where(resumed[:, None, None, None] > 0, ordered_blocks, resident_cache)
    context = attend_rows(queries, active_cache, token_keys, token_values, lengths)
    head_rows = lax.all_to_all(context, "ep", split_axis=1, concat_axis=0, tiled=True)
    projected = lax.psum_scatter(
        jnp.dot(head_rows, out_proj, preferred_element_type=jnp.float32),
        "ep",
        scatter_dimension=0,
        tiled=True,
    )
    attended = (residual.astype(jnp.float32) + projected).astype(jnp.bfloat16)
    widened = attended.astype(jnp.float32)
    normed = (
        widened
        * lax.rsqrt(jnp.mean(widened * widened, axis=-1, keepdims=True) + NORM_EPSILON)
        * norm_gain.astype(jnp.float32)
    ).astype(jnp.bfloat16)
    top_count = expert_ids.shape[1]
    capacity = min(total_rows, max(2, 2 * total_rows * top_count // expert_count))
    flat_ids = expert_ids.reshape(-1)
    hit_table = (flat_ids[:, None] == jnp.arange(expert_count)[None, :]).astype(jnp.int32)
    slot_rank = jnp.sum(jnp.cumsum(hit_table, axis=0) * hit_table, axis=1) - 1
    slot_index = flat_ids * capacity + slot_rank
    source_row = jnp.arange(total_rows * top_count) // top_count
    outgoing = (
        jnp.zeros((expert_count * capacity, D), jnp.bfloat16).at[slot_index].set(normed[source_row])
    )
    outgoing = outgoing.reshape(expert_count, capacity, D)
    w_gate = expert_gate[0]
    w_up = expert_up[0]
    w_down = expert_down[0]
    grouped = lax.all_gather(outgoing[None], "pool", axis=0, tiled=True)
    arrived_all = lax.all_to_all(grouped, "ep", split_axis=1, concat_axis=1, tiled=True)
    flat_tokens = arrived_all.reshape(-1, D)
    gate_part = jnp.dot(flat_tokens, w_gate, preferred_element_type=jnp.float32)
    up_part = jnp.dot(flat_tokens, w_up, preferred_element_type=jnp.float32)
    hidden = (jax.nn.silu(gate_part) * up_part).astype(jnp.bfloat16)
    partial_value = jnp.dot(hidden, w_down, preferred_element_type=jnp.float32)
    partials = partial_value.reshape(arrived_all.shape[:-1] + (D,))
    summed = lax.psum_scatter(
        partials.astype(jnp.bfloat16), "pool", scatter_dimension=0, tiled=True
    ).astype(jnp.float32)
    finished = summed[0].astype(jnp.bfloat16)
    returned = lax.all_to_all(finished, "ep", split_axis=0, concat_axis=0, tiled=True)
    flat_returned = returned.reshape(expert_count * capacity, D)
    picked = flat_returned[slot_index].reshape(total_rows, top_count, D)
    shares = route_scores / jnp.sum(route_scores, axis=1, keepdims=True)
    mixture = jnp.sum(shares[:, :, None] * picked.astype(jnp.float32), axis=1)
    layer_out = (widened + mixture).astype(jnp.bfloat16)
    return (attended, layer_out)


def solution(mesh):
    placed = (
        P(("pool", "ep"), None),
        P(("pool", "ep"), None),
        P(("pool", "ep"), None),
        P(("pool", "ep"), None),
        P(("pool", "ep"), None, None, None),
        P("ep", "pool", None, None, None),
        P(("pool", "ep"), None),
        P(("pool", "ep")),
        P(("pool", "ep")),
        P("ep", None),
        P(),
        P(("pool", "ep"), None),
        P(("pool", "ep"), None),
        P("ep", None, "pool"),
        P("ep", None, "pool"),
        P("ep", "pool", None),
    )
    return jax.shard_map(
        shards,
        mesh=mesh,
        in_specs=placed,
        out_specs=(P(("pool", "ep"), None), P(("pool", "ep"), None)),
        check_vma=False,
    )
```

profile of v0, /device:TPU:24, one launch (start us, length us, event | category | flops | bytes accessed | tf_op | source)
XLA Modules:
  0.0 612.3 jit_solution(1993379963594759516)
XLA Ops:
  7.2 0.0 all-gather.3.cloned.1.call-start
  7.2 0.7 all-gather.3.cloned.1.call-update
  7.9 0.0 all-reduce.3.cloned.1.call-start
  8.0 0.8 compare_and_fusion.1
  8.8 0.1 copy.49
  8.9 0.1 copy.50
  9.0 0.7 compare_select_fusion
  9.7 0.1 copy.52
  9.8 0.1 reshape.165
  9.9 0.7 bitcast_convert_fusion
  10.6 0.7 broadcast_compare_fusion
  11.2 0.7 iota_compare_fusion.1
  12.0 1.1 fusion.33
  13.0 48.5 %all-gather.3.cloned.1.call-done = bf16[1,128,2,16,512]{4,3,2,0,1:T(8,128)(2,1)} async-done(((bf16[1,32,2,16,512]{4,3,2,0,1:T(8,128)(2,1)}), bf16[1,128,2,16,512]{4,3,2,0,1:T(8,128)(2,1)}) %all-gather.3.cloned.1.call-update) | async-done | bytes 4194320 | tf_op jit(solution)/shard_map/all_gather | solution.py:80
  61.5 3.8 gather_fusion
  65.3 1.5 select_bitcast_fusion
  66.8 0.1 copy.53
  66.9 0.2 bitcast_select_fusion
  67.1 1.1 fusion.44
  68.2 2.0 reshape_squeeze.6
  70.1 1.5 fusion.45
  71.7 0.3 fusion.21
  72.0 2.0 reshape_squeeze.7
  74.0 1.4 fusion.13
  75.4 0.1 copy.58
  75.5 21.5 %all_to_all.26 = bf16[8,64,128]{2,0,1:T(8,128)(2,1)S(1)} all-to-all(bf16[8,64,128]{2,0,1:T(8,128)(2,1)S(1)} %copy.58), channel_id=1, replica_groups=mesh['pool'=4,'ep'=64] {'ep'}, dimensions={1} | all-to-all | bytes 262144 | tf_op jit(solution)/shard_map/all_to_all | solution.py:90
  97.0 5.7 fusion.26
  102.7 0.0 all-reduce.3.cloned.1.call-update
  102.7 0.0 all-gather.5.cloned.1.call-start
  102.8 0.6 copy-done.7
  103.4 0.1 eq.15
  103.5 0.1 mul.89
  103.5 0.6 dynamic-slice
  104.8 0.1 fusion.36
  104.9 0.1 reduce_window_sum.11
  105.0 0.2 select_reduce_fusion
  105.2 198.5 %all-reduce.3.cloned.1.call-done = f32[512,4096]{1,0:T(8,128)} async-done(((f32[512,4096]{1,0:T(8,128)}), f32[512,4096]{1,0:T(8,128)}) %all-reduce.3.cloned.1.call-update) | async-done | bytes 8388624
  303.7 1.1 fusion.22
  304.8 0.1 fusion.24
  304.9 4.0 scatter_custom_fusion
  308.8 2.5 broadcast_in_dim_reshape.4
  311.4 2.8 copy.59
  314.1 0.0 all-gather.5.cloned.1.call-update
  314.2 0.2 reduce-scatter.2.cloned.1.call-start
  314.4 47.6 %all-gather.5.cloned.1.call-done = bf16[4,64,2,4096]{3,1,2,0:T(8,128)(2,1)} async-done(((bf16[1,64,2,4096]{3,1,2,0:T(8,128)(2,1)}), bf16[4,64,2,4096]{3,1,2,0:T(8,128)(2,1)}) %all-gather.5.cloned.1.call-update) | async-done | bytes 4194320 | tf_op jit(solution)/shard_map/all_gather | solution.py:118
  362.0 8.5 %copy.60 = bf16[4,64,2,4096]{3,2,0,1:T(2,128)(2,1)} copy(bf16[4,64,2,4096]{3,1,2,0:T(8,128)(2,1)} %all-gather.5.cloned.1.call-done) | data formatting | bytes 8388608 | tf_op jit(solution)/shard_map/all_gather | solution.py:118
  370.6 107.1 %all_to_all.27 = bf16[4,64,2,4096]{3,2,0,1:T(2,128)(2,1)} all-to-all(bf16[4,64,2,4096]{3,2,0,1:T(2,128)(2,1)} %copy.60), channel_id=1, replica_groups=mesh['pool'=4,'ep'=64] {'ep'}, dimensions={1} | all-to-all | bytes 8388608 | tf_op jit(solution)/shard_map/all_to_all | solution.py:119
  477.6 9.7 %copy.61 = bf16[4,64,2,4096]{3,2,1,0:T(2,128)(2,1)} copy(bf16[4,64,2,4096]{3,2,0,1:T(2,128)(2,1)} %all_to_all.27) | data formatting | bytes 8388608 | tf_op jit(solution)/shard_map/all_to_all | solution.py:119
  487.4 7.2 %reshape.159 = bf16[512,4096]{1,0:T(8,128)(2,1)} reshape(bf16[4,64,2,4096]{3,2,1,0:T(2,128)(2,1)} %copy.61) | data formatting | bytes 8388608 | tf_op jit(solution)/shard_map/reshape | solution.py:120
  494.6 5.6 fusion.3
  500.2 3.1 fusion.8
  503.3 1.9 dot_general.29
  505.2 5.3 convolution_convert_fusion
  510.5 0.0 reduce-scatter.2.cloned.1.call-update
  510.5 44.5 %reduce-scatter.2.cloned.1.call-done = bf16[1,64,2,4096]{3,1,2,0:T(8,128)(2,1)} async-done(((bf16[4,64,2,4096]{3,1,2,0:T(8,128)(2,1)}), bf16[1,64,2,4096]{3,1,2,0:T(8,128)(2,1)}) %reduce-scatter.2.cloned.1.call-update) | async-done | bytes 1048592 | tf_op jit(solution)/shard_map/reduce_scatter | solution.py:126
  555.0 3.3 copy.63
  558.4 10.7 %all-to-all-start.2 = ((bf16[64,2,4096]{2,1,0:T(2,128)(2,1)}), bf16[64,2,4096]{2,1,0:T(2,128)(2,1)}, u32[]{:S(2)}, u32[]{:S(2)}) async-start(bf16[64,2,4096]{2,1,0:T(2,128)(2,1)} %copy.63), calls=%async_computation.3 | async-start | bytes 2097152 | tf_op jit(solution)/shard_map/all_to_all | solution.py:130
  569.1 0.1 reduce_sum.46
  569.2 0.1 broadcast_divide_fusion
  569.3 28.5 %all-to-all-done.2 = bf16[64,2,4096]{2,1,0:T(2,128)(2,1)} async-done(((bf16[64,2,4096]{2,1,0:T(2,128)(2,1)}), bf16[64,2,4096]{2,1,0:T(2,128)(2,1)}, u32[]{:S(2)}, u32[]{:S(2)}) %all-to-all-start.2) | async-done | bytes 1048608 | tf_op jit(solution)/shard_map/all_to_all | solution.py:130
  597.8 2.3 reshape.160
  600.1 3.5 gather_fusion.1
  603.6 1.5 fusion.14
  605.1 0.6 fusion.25
  (30 shorter events, 0.1 us)
Async XLA Ops:
  7.2 498.0 %copy-start = (bf16[1,384,4096]{2,1,0:T(8,128)(2,1)S(1)}, bf16[1,384,4096]{2,1,0:T(8,128)(2,1)}, u32[]{:S(2)}) copy-start(bf16[1,384,4096]{2,1,0:T(8,128)(2,1)} %param.31) | copy-start | bytes 9437188
  7.2 54.3 %all-gather.3.cloned.1.call-start = ((), (), s32[]{:S(2)}) async-start(), calls=%async_computation.4 | async-start | bytes 5242880 | tf_op jit(solution)/shard_map/all_gather | solution.py:80
  7.9 295.8 %all-reduce.3.cloned.1.call-start = ((), (), s32[]{:S(2)}) async-start(), calls=%async_computation.7 | async-start | bytes 16777216
  65.3 1.6 copy-start.2
  102.7 0.7 copy-start.7
  102.7 0.7 copy-start.6
  102.7 0.9 copy-start.9
  102.7 201.0 %copy-start.4 = (bf16[8,4096]{1,0:T(8,128)(2,1)S(1)}, bf16[8,4096]{1,0:T(8,128)(2,1)}, u32[]{:S(2)}) copy-start(bf16[8,4096]{1,0:T(8,128)(2,1)} %param.16) | copy-start | bytes 196612
  102.7 259.3 %all-gather.5.cloned.1.call-start = ((), (), s32[]{:S(2)}) async-start(), calls=%async_computation.5 | async-start | bytes 5242880 | tf_op jit(solution)/shard_map/all_gather | solution.py:118
  304.7 300.3 %copy-start.3 = (bf16[8,4096]{1,0:T(8,128)(2,1)}, bf16[8,4096]{1,0:T(8,128)(2,1)S(1)}, u32[]{:S(2)}) copy-start(bf16[8,4096]{1,0:T(8,128)(2,1)S(1)} %get-tuple-element.3) | copy-start | bytes 196612
  314.2 240.9 %reduce-scatter.2.cloned.1.call-start = ((), (), s32[]{:S(2)}) async-start(), calls=%async_computation.6 | async-start | bytes 5242880 | tf_op jit(solution)/shard_map/reduce_scatter | solution.py:126
  494.6 5.6 copy-start.1
  494.6 5.6 copy-start.8
  510.5 58.6 %copy-start.5 = (f32[8,8]{1,0:T(8,128)S(1)}, f32[8,8]{1,0:T(8,128)}, u32[]{:S(2)}) copy-start(f32[8,8]{1,0:T(8,128)} %param.28) | copy-start | bytes 772
  558.4 39.4 %all-to-all-start.2 = ((bf16[64,2,4096]{2,1,0:T(2,128)(2,1)}), bf16[64,2,4096]{2,1,0:T(2,128)(2,1)}, u32[]{:S(2)}, u32[]{:S(2)}) async-start(bf16[64,2,4096]{2,1,0:T(2,128)(2,1)} %copy.63), calls=%async_computation.3 | async-start | bytes 2097152 | tf_op jit(solution)/shard_map/all_to_all | solution.py:130
Sparse Core Ops, SparseCore 0:
  9.8 51.6 all-gather.2
  102.8 200.8 all-reduce.2
  314.3 47.7 all-gather.4
  510.6 44.3 reduce-scatter.1
where the time goes:
time: 616 us; the launch traced here: 612 us
  waiting for transfers between devices  368 us (60%)
  blocking collectives  129 us (21%)
  local copies, waits for them, and re-layouts  56.5 us (9%)
  matrix products  23.6 us (4%)
  between operations  14.6 us (2%)
  starting transfers between devices  11 us (2%)
  other arithmetic  9.48 us (2%)
    unnamed x5, waiting for transfers between devices  199 us
    all_to_all x1, blocking collectives, shards(): lax.all_to_all(grouped, 'ep', split_axis=1, concat_axis=1, tiled=True)  107 us
    all_gather x1, waiting for transfers between devices, shards(): shard_piece = lax.all_gather(pool_block_cache, 'pool', axis=1, tiled=True)  48.5 us
    all_gather x1, waiting for transfers between devices, shards(): grouped = lax.all_gather(outgoing[None], 'pool', axis=0, tiled=True)  47.6 us
    reduce_scatter x1, waiting for transfers between devices, shards(): lax.psum_scatter(partials.astype(jnp.bfloat16), 'pool', scatter_dimension...  44.5 us
    all_to_all x1, waiting for transfers between devices, shards(): lax.all_to_all(finished, 'ep', split_axis=0, concat_axis=0, tiled=True)  28.5 us
    all_to_all x1, blocking collectives, shards(): lax.all_to_all(context, 'ep', split_axis=1, concat_axis=0, tiled=True)  21.5 us
  transfers between devices with their start and end apart: 5, of which 5 were waited for; matrix products, arithmetic and copies ran while one was open for 1% of the time, Pallas kernels for 0%

commit v1 on v0

v1 whole, which is shorter than its diff:
```python
import functools
import math

import jax
import jax.numpy as jnp
import numpy as np
from jax import lax
from jax.experimental import pallas as pl
from jax.experimental.pallas import tpu as pltpu
from jax.sharding import PartitionSpec as P

D = 4096
QUERY_HEADS = 64
KEY_VALUE_HEADS = 4
GROUP = QUERY_HEADS // KEY_VALUE_HEADS
HEAD_SIZE = 128
WIDE = KEY_VALUE_HEADS * HEAD_SIZE
CONTEXT_LIMIT = 64
BLOCK_POSITIONS = 16
RES_MOST = 4
CAP = 2
ROWS = 8
FACTS = 7
N_POOL = 4
N_Z, N_X, N_CORE = 8, 4, 2
N_PLANE = N_X * N_CORE
N_EP = N_Z * N_PLANE
DEEP = N_PLANE * HEAD_SIZE
CHUNK = D // N_PLANE
PARTS = 4
PART = D // PARTS
FF_PART = 384
STEPS = 2
PER_STEP = PARTS // STEPS
HALF = N_EP // 2 * PARTS * CAP
NORM_EPSILON = 1e-06
NEG_FILL = -1e30
BIG = 48 * 1024 * 1024
MOST = 60 * 1024 * 1024


def shift_pool(value, step):
    return lax.ppermute(value, "pool", [(i, (i + step) % N_POOL) for i in range(N_POOL)])


def shift_ep(value, x=0, core=0):
    pairs = []
    for i in range(N_EP):
        a, b, c = i // N_PLANE, i // N_CORE % N_X, i % N_CORE
        pairs.append((i, a * N_PLANE + (b + x) % N_X * N_CORE + (c + core) % N_CORE))
    return lax.ppermute(value, "ep", pairs)


def whole(shape):
    return pl.BlockSpec(shape, lambda *_: (0,) * len(shape))


def gather_kernel(asked_ref, cache_ref, *refs):
    outs, sems = refs[:N_POOL], refs[N_POOL]
    copies = []
    for d in range(N_POOL):
        for j in range(RES_MOST):
            copy = pltpu.make_async_copy(
                cache_ref.at[asked_ref[d * RES_MOST + j]], outs[d].at[j], sems.at[d * RES_MOST + j]
            )
            copy.start()
            copies.append(copy)
    for copy in copies:
        copy.wait()


def fetch_blocks(cache, block_table, resumed, lengths, pool):
    slots = cache.shape[0]
    live = resumed > 0
    row = jnp.arange(ROWS)
    rank = jnp.sum(jnp.where(row[None, :] < row[:, None], resumed[None, :], 0), axis=1)
    rank = jnp.clip(rank, 0, RES_MOST - 1)
    holder = block_table // slots
    within = block_table % slots
    from_me = (pool + jnp.arange(N_POOL)) % N_POOL
    at_holder = holder[None] == from_me[:, None, None]
    at_rank = live[None, :] & (rank[None, :] == jnp.arange(RES_MOST)[:, None])
    chosen = at_holder[:, None] & at_rank[None, :, :, None]
    wanted = jnp.sum(jnp.where(chosen, within[None, None], 0), axis=(2, 3))
    start = jnp.arange(N_POOL) * BLOCK_POSITIONS
    place = jnp.sum(jnp.where(at_holder, start[None, None, :], 0), axis=2).T
    place = jnp.where(live[:, None], place, start[None, :])
    asked = jnp.concatenate([wanted[0]] + [shift_pool(wanted[d], d) for d in range(1, N_POOL)])
    asked = jnp.clip(asked, 0, slots - 1)
    shape = jax.ShapeDtypeStruct((RES_MOST,) + cache.shape[1:], jnp.bfloat16)
    gathered = pl.pallas_call(
        gather_kernel,
        grid_spec=pltpu.PrefetchScalarGridSpec(
            num_scalar_prefetch=1,
            grid=(1,),
            in_specs=[pl.BlockSpec(memory_space=pl.ANY)],
            out_specs=[whole((RES_MOST,) + cache.shape[1:])] * N_POOL,
            scratch_shapes=[pltpu.SemaphoreType.DMA((N_POOL * RES_MOST,))],
        ),
        out_shape=[shape] * N_POOL,
        cost_estimate=pl.CostEstimate(flops=0, bytes_accessed=1 << 20, transcendentals=0),
    )(asked, cache)
    blocks = [gathered[0]] + [shift_pool(gathered[d], -d) for d in range(1, N_POOL)]
    facts = jnp.concatenate([rank[:, None], resumed[:, None], lengths[:, None], place], axis=1)
    return blocks, facts.reshape(-1)


def attention_kernel(facts_ref, query_ref, key_ref, value_ref, resident_ref, b0, b1, b2, b3, out_ref):
    wider = CONTEXT_LIMIT + 16
    lane = lax.broadcasted_iota(jnp.int32, (1, wider), 1)
    head_of = lax.broadcasted_iota(jnp.int32, (QUERY_HEADS, WIDE), 0) // GROUP
    block_of = lax.broadcasted_iota(jnp.int32, (QUERY_HEADS, WIDE), 1) // HEAD_SIZE
    diagonal = head_of == block_of
    first = lax.broadcasted_iota(jnp.int32, (16, WIDE), 0) == 0
    factor = 1.0 / math.sqrt(HEAD_SIZE)
    results = []
    for row in range(ROWS):
        rank, resumed, length, *place = [facts_ref[row * FACTS + i] for i in range(FACTS)]
        is_resumed = resumed > 0

        def of_kind(kind, own_ref):
            loaded = jnp.concatenate([b[rank, kind] for b in (b0, b1, b2, b3)], axis=0)
            cached = jnp.where(is_resumed, loaded, resident_ref[row, kind])
            own = jnp.where(first, own_ref[row : row + 1, :].astype(jnp.float32), 0.0)
            return jnp.concatenate([cached, own.astype(jnp.bfloat16)], axis=0)

        keys, values = of_kind(0, key_ref), of_kind(1, value_ref)
        position = lane % BLOCK_POSITIONS
        for i in range(N_POOL):
            position = position + jnp.where(lane // BLOCK_POSITIONS == i, place[i], 0)
        live = ((lane < CONTEXT_LIMIT) & (position < length)) | (lane == CONTEXT_LIMIT)
        query = query_ref[row]
        query = jnp.where(diagonal, jnp.concatenate([query] * KEY_VALUE_HEADS, axis=1), 0)
        scores = lax.dot_general(
            query.astype(jnp.bfloat16), keys, (((1,), (1,)), ((), ())), preferred_element_type=jnp.float32
        )
        scores = jnp.where(live, scores * factor, NEG_FILL)
        highest = jnp.max(scores, axis=1, keepdims=True)
        raised = jnp.where(live, jnp.exp(scores - highest), 0.0)
        weights = (raised / jnp.sum(raised, axis=1, keepdims=True)).astype(jnp.bfloat16)
        spread = jnp.dot(weights, values, preferred_element_type=jnp.float32)
        results.append(
            jnp.concatenate(
                [
                    spread[k * GROUP : (k + 1) * GROUP, k * HEAD_SIZE : (k + 1) * HEAD_SIZE]
                    for k in range(KEY_VALUE_HEADS)
                ],
                axis=0,
            )
        )
    by_head = jnp.swapaxes(jnp.stack(results), 0, 1)
    for z in range(N_Z):
        plane = jnp.concatenate([by_head[z * N_PLANE + h] for h in range(N_PLANE)], axis=1)
        copies = jnp.concatenate([plane] * N_X, axis=0).astype(jnp.bfloat16)
        out_ref[z * N_X * ROWS : (z + 1) * N_X * ROWS, :] = copies


def attend(queries, token_keys, token_values, resident, blocks, facts):
    block = whole(blocks[0].shape)
    sent = N_Z * N_X * ROWS
    return pl.pallas_call(
        attention_kernel,
        grid_spec=pltpu.PrefetchScalarGridSpec(
            num_scalar_prefetch=1,
            grid=(1,),
            in_specs=[
                whole((ROWS, QUERY_HEADS, HEAD_SIZE)),
                whole((ROWS, WIDE)),
                whole((ROWS, WIDE)),
                whole(resident.shape),
                block,
                block,
                block,
                block,
            ],
            out_specs=whole((sent, DEEP)),
        ),
        out_shape=jax.ShapeDtypeStruct((sent, DEEP), jnp.bfloat16),
        compiler_params=pltpu.CompilerParams(vmem_limit_bytes=MOST),
        cost_estimate=pl.CostEstimate(flops=1 << 28, bytes_accessed=3 << 20, transcendentals=1 << 16),
    )(
        facts, queries.reshape(ROWS, QUERY_HEADS, HEAD_SIZE), token_keys, token_values, resident, *blocks
    )


def pair_projection(out_proj, core):
    columns = N_X * CHUNK
    mine = lax.dynamic_slice_in_dim(out_proj, core * columns, columns, 1)
    other = lax.dynamic_slice_in_dim(out_proj, (1 - core) * columns, columns, 1)
    came = shift_ep(other, core=1)
    both = jnp.where(core == 0, jnp.stack([mine, came]), jnp.stack([came, mine]))
    return both.reshape(N_CORE * HEAD_SIZE, columns)


def spread_projection(pair, x):
    pieces = []
    for d in range(N_X):
        piece = lax.dynamic_slice_in_dim(pair, (x + d) % N_X * CHUNK, CHUNK, 1)
        pieces.append(piece if d == 0 else shift_ep(piece, x=d))
    return pieces


def project_kernel(at_ref, mine_ref, other_ref, w0, w1, w2, w3, out_ref):
    x, core = at_ref[0], at_ref[1]
    width = N_CORE * HEAD_SIZE
    products = []
    for rows_ref in (mine_ref, other_ref):
        total = jnp.zeros((rows_ref.shape[0], CHUNK), jnp.float32)
        for d, w_ref in enumerate((w0, w1, w2, w3)):
            source = (x + N_X - d) % N_X
            columns = pl.ds(pl.multiple_of(source * width, width), width)
            total = total + jnp.dot(rows_ref[:, columns], w_ref[...], preferred_element_type=jnp.float32)
        products.append(total.reshape(N_Z * N_X, ROWS, CHUNK))
    mine, other = products
    first = jnp.where(core == 0, mine, other)
    second = jnp.where(core == 0, other, mine)
    both = jnp.concatenate([first, second], axis=1)
    out_ref[...] = both.reshape(N_EP * ROWS, CHUNK).astype(jnp.bfloat16)


def project(context, pieces, x, core):
    same_core = [[i * N_CORE + c for i in range(N_Z * N_X)] for c in range(N_CORE)]
    mine = lax.all_to_all(
        context.reshape(N_Z * N_X, ROWS, DEEP),
        "ep", split_axis=0, concat_axis=0, axis_index_groups=same_core, tiled=True,
    ).reshape(N_Z * N_X * ROWS, DEEP)
    other = shift_ep(mine, core=1)
    product = pl.pallas_call(
        project_kernel,
        grid_spec=pltpu.PrefetchScalarGridSpec(
            num_scalar_prefetch=1,
            grid=(1,),
            in_specs=[whole(mine.shape)] * 2 + [whole(pieces[0].shape)] * N_X,
            out_specs=whole((N_EP * ROWS, CHUNK)),
        ),
        out_shape=jax.ShapeDtypeStruct((N_EP * ROWS, CHUNK), jnp.bfloat16),
        compiler_params=pltpu.CompilerParams(vmem_limit_bytes=BIG),
    )(jnp.stack([x, core]).astype(jnp.int32), mine, other, *pieces)
    summands = lax.all_to_all(
        product.reshape(N_EP, ROWS, CHUNK), "ep", split_axis=0, concat_axis=0, tiled=True
    )
    return summands.reshape(N_EP * ROWS, CHUNK)


def dispatch_kernel(summand_ref, residual_ref, gain_ref, pick_ref, attended_ref, out_ref):
    total = summand_ref[...].astype(jnp.float32).reshape(N_Z, N_PLANE * ROWS, CHUNK).sum(axis=0)
    columns = []
    for chunk in range(N_PLANE):
        source = chunk % N_X * N_CORE + chunk // N_X
        columns.append(total[source * ROWS : (source + 1) * ROWS])
    projected = jnp.concatenate(columns, axis=1)
    attended = (residual_ref[...].astype(jnp.float32) + projected).astype(jnp.bfloat16)
    attended_ref[...] = attended
    widened = attended.astype(jnp.float32)
    mean = jnp.sum(widened * widened, axis=1, keepdims=True) * (1.0 / D)
    normed = widened * lax.rsqrt(mean + NORM_EPSILON) * gain_ref[...].astype(jnp.float32)
    stacked = jnp.concatenate([normed[:, j * PART : (j + 1) * PART] for j in range(PARTS)], axis=0)
    out_ref[...] = jnp.dot(
        pick_ref[...], stacked.astype(jnp.bfloat16), preferred_element_type=jnp.float32
    ).astype(jnp.bfloat16)


def expert_kernel(layout, order_ref, *refs):
    count = len(layout)
    ins, (gate_ref, up_ref, down_ref) = refs[:count], refs[count : count + 3]
    outs = refs[count + 3 : 2 * count + 3]
    tokens, gate_sum, up_sum, hidden, results = refs[2 * count + 3 :]
    halves = [(i, h) for i, n in enumerate(layout) for h in range(n)]
    per_half = HALF // PARTS
    step = pl.program_id(0)

    @pl.when(step == 0)
    def _():
        for at, (i, h) in enumerate(halves):
            block = jnp.dot(
                order_ref[...], ins[i][h * HALF : (h + 1) * HALF, :], preferred_element_type=jnp.float32
            ).astype(jnp.bfloat16)
            for j in range(PARTS):
                tokens[j, at * per_half : (at + 1) * per_half, :] = block[j * per_half : (j + 1) * per_half]

    for i in range(STEPS):

        @pl.when(step == i)
        def _():
            gate = up = None
            for at in range(PER_STEP):
                part = tokens[i * PER_STEP + at]
                depth = slice(at * PART, (at + 1) * PART)
                more = jnp.dot(part, gate_ref[depth, :], preferred_element_type=jnp.float32)
                gate = more if gate is None else gate + more
                more = jnp.dot(part, up_ref[depth, :], preferred_element_type=jnp.float32)
                up = more if up is None else up + more
            if i > 0:
                gate, up = gate + gate_sum[...], up + up_sum[...]
            if i < STEPS - 1:
                gate_sum[...], up_sum[...] = gate, up
            else:
                hidden[...] = (gate * (1.0 / (1.0 + jnp.exp(-gate))) * up).astype(jnp.bfloat16)

        @pl.when(step == STEPS + i)
        def _():
            for at in range(PER_STEP):
                results[i * PER_STEP + at] = jnp.dot(
                    hidden[...], down_ref[:, at * PART : (at + 1) * PART], preferred_element_type=jnp.float32
                ).astype(jnp.bfloat16)

    @pl.when(step == 2 * STEPS - 1)
    def _():
        for at, (i, h) in enumerate(halves):
            block = jnp.concatenate(
                [results[j, at * per_half : (at + 1) * per_half, :] for j in range(PARTS)], axis=0
            )
            outs[i][h * HALF : (h + 1) * HALF, :] = lax.dot_general(
                order_ref[...], block, (((0,), (0,)), ((), ())), preferred_element_type=jnp.float32
            ).astype(jnp.bfloat16)


def expert(arrays, w_gate, w_up, w_down, order):
    layout = [a.shape[0] // HALF for a in arrays]
    rows = sum(layout) * HALF // PARTS
    span = PER_STEP * PART
    gate_spec = pl.BlockSpec((span, FF_PART), lambda i: (jnp.minimum(i, STEPS - 1), 0))
    down_spec = pl.BlockSpec((FF_PART, span), lambda i: (0, jnp.maximum(i - STEPS, 0)))
    return pl.pallas_call(
        functools.partial(expert_kernel, layout),
        grid=(2 * STEPS,),
        in_specs=[whole(order.shape)] + [whole(a.shape) for a in arrays] + [gate_spec, gate_spec, down_spec],
        out_specs=[whole(a.shape) for a in arrays],
        out_shape=[jax.ShapeDtypeStruct(a.shape, jnp.bfloat16) for a in arrays],
        scratch_shapes=[
            pltpu.VMEM((PARTS, rows, PART), jnp.bfloat16),
            pltpu.VMEM((rows, FF_PART), jnp.float32),
            pltpu.VMEM((rows, FF_PART), jnp.float32),
            pltpu.VMEM((rows, FF_PART), jnp.bfloat16),
            pltpu.VMEM((PARTS, rows, PART), jnp.bfloat16),
        ],
        compiler_params=pltpu.CompilerParams(vmem_limit_bytes=BIG),
        cost_estimate=pl.CostEstimate(
            flops=6 * rows * D * FF_PART, bytes_accessed=6 * D * FF_PART + 4 * rows * D, transcendentals=0
        ),
    )(order, *arrays, w_gate, w_up, w_down)


def finish_kernel(mix_ref, returned_ref, attended_ref, out_ref):
    summed = jnp.dot(mix_ref[...], returned_ref[...], preferred_element_type=jnp.float32)
    wide = PARTS * ROWS
    summed = summed[:wide] + summed[wide : 2 * wide] + summed[2 * wide :]
    mixture = jnp.concatenate([summed[j * ROWS : (j + 1) * ROWS] for j in range(PARTS)], axis=1)
    out_ref[...] = (attended_ref[...].astype(jnp.float32) + mixture).astype(jnp.bfloat16)


def routes(expert_ids, route_scores):
    shares = route_scores / jnp.sum(route_scores, axis=1, keepdims=True)
    named = expert_ids[:, :, None] == jnp.arange(N_EP)[None, None, :]
    hit = jnp.any(named, axis=1)
    share = jnp.sum(jnp.where(named, shares[:, :, None], 0.0), axis=1)
    row = jnp.arange(ROWS)
    earlier = row[None, :, None] < row[:, None, None]
    before = jnp.sum(jnp.where(earlier & hit[None], 1, 0), axis=1)
    slot = hit[:, :, None] & (before[:, :, None] == jnp.arange(CAP))
    same = jnp.arange(PARTS)[:, None] == jnp.arange(PARTS)[None, :]
    pick = jnp.where(
        slot.transpose(1, 2, 0)[:, None, :, None, :] & same[None, :, None, :, None], 1.0, 0.0
    ).reshape(N_EP * PARTS * CAP, PARTS * ROWS)
    mix = jnp.where(
        slot[None, :, :, None, :] & same[:, None, None, :, None], share[None, :, :, None, None], 0.0
    ).reshape(PARTS * ROWS, N_EP * PARTS * CAP)
    high = lax.reduce_precision(mix, 8, 7)
    middle = lax.reduce_precision(mix - high, 8, 7)
    low = mix - high - middle
    return pick.astype(jnp.bfloat16), jnp.concatenate([high, middle, low]).astype(jnp.bfloat16)


def order_matrix():
    half = N_EP // 2
    message = np.arange(HALF).reshape(half, PARTS, CAP)
    token = message.transpose(1, 0, 2).reshape(-1)
    return (token[:, None] == np.arange(HALF)[None, :]).astype(jnp.bfloat16)


def shards(
    residual,
    queries,
    token_keys,
    token_values,
    resident_cache,
    pool_block_cache,
    block_table,
    resumed,
    lengths,
    out_proj,
    norm_gain,
    expert_ids,
    route_scores,
    expert_gate,
    expert_up,
    expert_down,
):
    pool = lax.axis_index("pool")
    ep = lax.axis_index("ep")
    x, core = ep // N_CORE % N_X, ep % N_CORE

    blocks, facts = fetch_blocks(pool_block_cache[0], block_table, resumed, lengths, pool)
    pair = pair_projection(out_proj, core)
    blocks[1], pair = lax.optimization_barrier((blocks[1], pair))
    pieces = spread_projection(pair, x)
    pick, mix = routes(expert_ids, route_scores)
    context = attend(queries, token_keys, token_values, resident_cache, blocks, facts)
    context, *pieces = lax.optimization_barrier((context, *pieces))
    summands = project(context, pieces, x, core)
    message = (N_EP * PARTS * CAP, PART)
    attended, outgoing = pl.pallas_call(
        dispatch_kernel,
        out_shape=[
            jax.ShapeDtypeStruct((ROWS, D), jnp.bfloat16),
            jax.ShapeDtypeStruct(message, jnp.bfloat16),
        ],
        compiler_params=pltpu.CompilerParams(vmem_limit_bytes=BIG),
    )(summands, residual, norm_gain.reshape(1, D), pick)

    def exchange(rows):
        parted = rows.reshape(N_EP, PARTS * CAP, PART)
        return lax.all_to_all(parted, "ep", split_axis=0, concat_axis=0, tiled=True).reshape(message)

    weights = (expert_gate[0], expert_up[0], expert_down[0], jnp.asarray(order_matrix()))
    mine = exchange(outgoing)
    left, right = shift_pool(mine, 1), shift_pool(mine, -1)
    (own,) = expert([mine], *weights)
    left, right, own = lax.optimization_barrier((left, right, own))
    far_a, far_b = shift_pool(right[:HALF], -1), shift_pool(left[HALF:], 1)
    to_left, to_right = expert([left, right], *weights)
    right_b, left_a = shift_pool(to_right[HALF:], 1), shift_pool(to_left[:HALF], -1)
    far_a, far_b, to_left, to_right = lax.optimization_barrier((far_a, far_b, to_left, to_right))
    to_far_a, to_far_b = expert([far_a, far_b], *weights)
    over_a, over_b = shift_pool(to_far_a, 1), shift_pool(to_far_b, -1)

    def wide(value):
        return value.astype(jnp.float32)

    base_a, base_b = wide(own[:HALF]) + wide(left_a), wide(own[HALF:]) + wide(right_b)
    over_a, over_b, base_a, base_b = lax.optimization_barrier((over_a, over_b, base_a, base_b))
    right_a = shift_pool((wide(to_right[:HALF]) + wide(over_a)).astype(jnp.bfloat16), 1)
    left_b = shift_pool((wide(to_left[HALF:]) + wide(over_b)).astype(jnp.bfloat16), -1)
    summed = jnp.concatenate([base_a + wide(right_a), base_b + wide(left_b)]).astype(jnp.bfloat16)
    returned = exchange(summed)
    layer_out = pl.pallas_call(
        finish_kernel,
        out_shape=jax.ShapeDtypeStruct((ROWS, D), jnp.bfloat16),
        compiler_params=pltpu.CompilerParams(vmem_limit_bytes=BIG),
    )(mix, returned, attended)
    return (attended, layer_out)


def solution(mesh):
    placed = (
        P(("pool", "ep"), None),
        P(("pool", "ep"), None),
        P(("pool", "ep"), None),
        P(("pool", "ep"), None),
        P(("pool", "ep"), None, None, None),
        P("ep", "pool", None, None, None),
        P(("pool", "ep"), None),
        P(("pool", "ep")),
        P(("pool", "ep")),
        P("ep", None),
        P(),
        P(("pool", "ep"), None),
        P(("pool", "ep"), None),
        P("ep", None, "pool"),
        P("ep", None, "pool"),
        P("ep", "pool", None),
    )
    return jax.shard_map(
        shards,
        mesh=mesh,
        in_specs=placed,
        out_specs=(P(("pool", "ep"), None), P(("pool", "ep"), None)),
        check_vma=False,
    )
```

time: 616 us -> 241 us (0.39)
  waiting for transfers between devices: 368 us -> 93.9 us
  blocking collectives: 129 us -> 59.3 us
  local copies, waits for them, and re-layouts: 56.5 us -> 7.02 us
  Pallas kernels: 0 us -> 32.3 us
  starting transfers between devices: 11 us -> 39.2 us
  matrix products: 23.6 us -> 0 us
  between operations: 14.6 us -> 0.99 us
    unnamed x5 -> x0, waiting for transfers between devices: 199 us -> none
    all_gather x2 -> x0, waiting for transfers between devices: 96.1 us -> none  [the longest x1 48.5 us: shards(): shard_piece = lax.all_gather(pool_block_cache, 'pool', axis=1, tiled=True)]
    all_to_all x2, blocking collectives: 129 us -> 59.3 us  [the longest x1 34.5 us: exchange(): lax.all_to_all(parted, 'ep', split_axis=0, concat_axis=0, tiled=True)]
    ppermute x0 -> x21, waiting for transfers between devices: none -> 52.6 us  [the longest x16 48.7 us: shift_pool(): lax.ppermute(value, 'pool', [(i, (i + step) % N_POOL) for i in range(N_PO...]
    reduce_scatter x1 -> x0, waiting for transfers between devices: 44.5 us -> none  [shards(): lax.psum_scatter(partials.astype(jnp.bfloat16), 'pool', scatter_dimension...]
    pallas_call x0 -> x8, Pallas kernels: none -> 32.3 us  [the longest x3 20.1 us: expert(): pl.pallas_call(functools.partial(expert_kernel, layout), grid=(2 * STEPS,...]
    ppermute x0 -> x21, starting transfers between devices: none -> 25.5 us  [the longest x16 22.6 us: shift_pool(): lax.ppermute(value, 'pool', [(i, (i + step) % N_POOL) for i in range(N_PO...]
    dot_general x7 -> x0, matrix products: 23.6 us -> none  [the longest x1 5.68 us: shards(): jnp.dot(head_rows, out_proj, preferred_element_type=jnp.float32)]
  transfers between devices with their start and end apart: 5 -> 23, of which waited for: 5 -> 16; matrix products, arithmetic and copies ran while one was open for 1% -> 4% of each run, Pallas kernels for 0% -> 12%
where the time goes in v1:
time: 241 us
  waiting for transfers between devices  93.9 us (39%)
  blocking collectives  59.3 us (25%)
  starting transfers between devices  39.2 us (16%)
  Pallas kernels  32.3 us (13%)
  other arithmetic  7.95 us (3%)
  local copies, waits for them, and re-layouts  7.02 us (3%)
    ppermute x16, waiting for transfers between devices, shift_pool(): lax.ppermute(value, 'pool', [(i, (i + step) % N_POOL) for i in range(N_PO...  48.7 us
    all_to_all x1, blocking collectives, exchange(): lax.all_to_all(parted, 'ep', split_axis=0, concat_axis=0, tiled=True)  34.5 us
    all_to_all x1, waiting for transfers between devices, exchange(): lax.all_to_all(parted, 'ep', split_axis=0, concat_axis=0, tiled=True)  27.2 us
    all_to_all x1, blocking collectives, project(): lax.all_to_all(context.reshape(N_Z * N_X, ROWS, DEEP), 'ep', split_axis=0...  24.8 us
    ppermute x16, starting transfers between devices, shift_pool(): lax.ppermute(value, 'pool', [(i, (i + step) % N_POOL) for i in range(N_PO...  22.6 us
    pallas_call x3, Pallas kernels, expert(): pl.pallas_call(functools.partial(expert_kernel, layout), grid=(2 * STEPS,...  20.1 us
    all_to_all x1, waiting for transfers between devices, project(): lax.all_to_all(product.reshape(N_EP, ROWS, CHUNK), 'ep', split_axis=0, co...  14.1 us
    all_to_all x1, starting transfers between devices, exchange(): lax.all_to_all(parted, 'ep', split_axis=0, concat_axis=0, tiled=True)  7.68 us
  transfers between devices with their start and end apart: 23, of which 16 were waited for; matrix products, arithmetic and copies ran while one was open for 4% of the time, Pallas kernels for 12%

profile of v1, /device:TPU:24, one launch (start us, length us, event | category | flops | bytes accessed | tf_op | source)
XLA Modules:
  0.0 240.6 jit_solution(7201275150980734781)
XLA Ops:
  0.7 1.3 dynamic-slice_bitcast_fusion
  2.1 0.7 broadcast_compare_fusion.2
  2.7 0.8 select_reduce_fusion.4
  3.5 0.7 add_select_fusion
  4.3 0.4 select_reduce_fusion.2
  4.7 0.8 collective-permute-start.2
  5.5 2.7 %collective-permute-start.1 = (s32[4]{0:T(128)S(1)}, s32[4]{0:T(128)S(1)}, u32[]{:S(2)}, u32[]{:S(2)}) collective-permute-start(s32[4]{0:T(128)S(1)} %get-tuple-element.73), channel_id=1, source_target_pairs={{0,128},{64,192},{128,0},{192,64},{1,129},{65,193},{129,1},{193,65... | collective-permute-start | bytes 56 | tf_op jit(solution)/shard_map/ppermute | solution.py:43
  8.2 0.4 collective-permute-start
  8.7 0.9 collective-permute-done.2
  9.5 1.0 collective-permute-done.1
  10.6 1.2 collective-permute-done
  11.8 0.7 add_clamp_fusion.asked_ref
  12.4 2.6 %shard_map.176 = (bf16[4,2,16,512]{3,2,1,0:T(8,128)(2,1)}, bf16[4,2,16,512]{3,2,1,0:T(8,128)(2,1)}, bf16[4,2,16,512]{3,2,1,0:T(8,128)(2,1)}, bf16[4,2,16,512]{3,2,1,0:T(8,128)(2,1)}) custom-call(s32[16]{0:T(128)} %add_clamp_fusion.asked_ref, bf16[32,2,16,512]{3,2,1,0:T(8,128)(2,1)} %bitcast.60), custom_call_target="tpu_custom_call" | custom-call | bytes 1048576 | tf_op jit(solution)/shard_map/pallas_call | solution.py:91
  15.0 0.8 collective-permute-start.3
  15.8 2.4 %collective-permute-start.5 = (bf16[4,2,16,512]{3,2,1,0:T(8,128)(2,1)}, bf16[4,2,16,512]{3,2,1,0:T(8,128)(2,1)S(1)}, u32[]{:S(2)}, u32[]{:S(2)}) collective-permute-start(bf16[4,2,16,512]{3,2,1,0:T(8,128)(2,1)} %get-tuple-element.33), channel_id=1, source_target_pairs={{0,128},{64,192},{128,0},{192,64},{1,129},{65,193},{129,1},{193,65... | collective-permute-start | bytes 393224 | tf_op jit(solution)/shard_map/ppermute | solution.py:43
  18.2 1.0 collective-permute-start.6
  19.3 0.2 maximum_select_fusion
  19.5 4.1 %collective-permute-done.3.b1 = bf16[4,2,16,512]{3,2,1,0:T(8,128)(2,1)S(1)} collective-permute-done((bf16[4,2,16,512]{3,2,1,0:T(8,128)(2,1)}, bf16[4,2,16,512]{3,2,1,0:T(8,128)(2,1)S(1)}, u32[]{:S(2)}, u32[]{:S(2)}) %collective-permute-start.3) | collective-permute-done | bytes 131104 | tf_op jit(solution)/shard_map/ppermute | solution.py:43
  23.6 1.1 collective-permute-start.9
  24.7 0.9 collective-permute-start.8
  25.6 0.9 collective-permute-start.7
  26.7 0.7 reshape.194.facts_ref
  27.3 0.7 copy.48
  28.0 0.6 copy-done.7
  28.7 5.6 %shard_map.177 = bf16[256,1024]{1,0:T(8,128)(2,1)} custom-call(s32[56]{0:T(128)} %reshape.194.facts_ref, bf16[8,64,128]{2,1,0:T(8,128)(2,1)} %bitcast.62, bf16[8,512]{1,0:T(8,128)(2,1)} %key_ref.1, bf16[8,512]{1,0:T(8,128)(2,1)} %value_ref.1, bf16[8,2,64,512]{3,2,1,0:T(8,128)(2,1)} %resident_ref.1, bf16[4,2,16,512]{3,2,1,0:T(8,128)(2,1)} %get-tuple-element.30.b0, ...), custom_call_target="tpu_custom_call" | custom-call | flops 268435456 | bytes 3145728 | tf_op jit(solution)/shard_map/pallas_call | solution.py:161
  34.4 2.0 collective-permute-done.7.w1
  36.4 24.8 %all_to_all.20 = bf16[32,8,1024]{2,1,0:T(8,128)(2,1)S(1)} all-to-all(bf16[32,8,1024]{2,1,0:T(8,128)(2,1)} %bitcast.59), channel_id=1, replica_groups={{0,2,4,6,8,10,12,14,16,18,20,22,24,26,28,30,32,34,36,38,40,42,44,46,48,..., dimensions={0} | all-to-all | bytes 1048576 | tf_op jit(solution)/shard_map/all_to_all | solution.py:223
  61.3 1.8 collective-permute-done.10.other_ref
  63.1 1.3 shard_map.178
  64.4 0.8 copy-done.2
  65.2 5.9 %all-to-all-start.1 = ((bf16[64,8,512]{2,1,0:T(8,128)(2,1)}), bf16[64,8,512]{2,1,0:T(8,128)(2,1)}, u32[]{:S(2)}, u32[]{:S(2)}) async-start(bf16[64,8,512]{2,1,0:T(8,128)(2,1)} %bitcast.48), calls=%async_computation.1 | async-start | bytes 1048576 | tf_op jit(solution)/shard_map/all_to_all | solution.py:239
  71.7 1.2 select_convert_fusion
  72.9 1.4 convert_element_type.48.pick_ref
  74.3 14.1 %all-to-all-done.1 = bf16[64,8,512]{2,1,0:T(8,128)(2,1)} async-done(((bf16[64,8,512]{2,1,0:T(8,128)(2,1)}), bf16[64,8,512]{2,1,0:T(8,128)(2,1)}, u32[]{:S(2)}, u32[]{:S(2)}) %all-to-all-start.1) | async-done | bytes 524320 | tf_op jit(solution)/shard_map/all_to_all | solution.py:239
  88.5 1.8 shard_map.179
  90.2 34.5 %all_to_all.21 = bf16[64,8,1024]{2,1,0:T(8,128)(2,1)S(1)} all-to-all(bf16[64,8,1024]{2,1,0:T(8,128)(2,1)S(1)} %bitcast.51), channel_id=1, replica_groups=mesh['pool'=4,'ep'=64] {'ep'}, dimensions={0} | all-to-all | bytes 2097152 | tf_op jit(solution)/shard_map/all_to_all | solution.py:423
  124.8 3.2 %collective-permute-start.11 = (bf16[512,1024]{1,0:T(8,128)(2,1)S(1)}, bf16[512,1024]{1,0:T(8,128)(2,1)S(1)}, u32[]{:S(2)}, u32[]{:S(2)}) collective-permute-start(bf16[512,1024]{1,0:T(8,128)(2,1)S(1)} %bitcast.45), channel_id=1, source_target_pairs={{0,64},{64,128},{128,192},{192,0},{1,65},{65,129},{129,193},{193,1... | collective-permute-start | bytes 3145736 | tf_op jit(solution)/shard_map/ppermute | solution.py:43
  127.9 5.9 %shard_map.180 = bf16[512,1024]{1,0:T(8,128)(2,1)S(1)} custom-call(bf16[256,256]{1,0:T(8,128)(2,1)S(1)} %copy-done.3, bf16[512,1024]{1,0:T(8,128)(2,1)S(1)} %bitcast.46, bf16[4096,384]{1,0:T(8,128)(2,1)S(1)} %bitcast.42, bf16[4096,384]{1,0:T(8,128)(2,1)} %bitcast.52, bf16[384,4096]{1,0:T(8,128)(2,1)} %bitcast.55), custom_call_target="tpu_custom_call" | custom-call | flops 1207959552 | bytes 11534336 | tf_op jit(solution)/shard_map/pallas_call | solution.py:324
  133.8 16.3 %collective-permute-done.12.refs_1_ = bf16[512,1024]{1,0:T(8,128)(2,1)S(1)} collective-permute-done((bf16[512,1024]{1,0:T(8,128)(2,1)S(1)}, bf16[512,1024]{1,0:T(8,128)(2,1)S(1)}, u32[]{:S(2)}, u32[]{:S(2)}) %collective-permute-start.12) | collective-permute-done | bytes 1048608 | tf_op jit(solution)/shard_map/ppermute | solution.py:43
  150.2 3.0 %collective-permute-start.14 = (bf16[256,1024]{1,0:T(8,128)(2,1)S(1)}, bf16[256,1024]{1,0:T(8,128)(2,1)S(1)}, u32[]{:S(2)}, u32[]{:S(2)}) collective-permute-start(bf16[256,1024]{1,0:T(8,128)(2,1)S(1)} %slice.41), channel_id=1, source_target_pairs={{0,64},{64,128},{128,192},{192,0},{1,65},{65,129},{129,193},{193,1... | collective-permute-start | bytes 1572872 | tf_op jit(solution)/shard_map/ppermute | solution.py:43
  153.2 8.3 %shard_map.181 = (bf16[512,1024]{1,0:T(8,128)(2,1)S(1)}, bf16[512,1024]{1,0:T(8,128)(2,1)S(1)}) custom-call(bf16[256,256]{1,0:T(8,128)(2,1)S(1)} %copy-done.3, bf16[512,1024]{1,0:T(8,128)(2,1)S(1)} %collective-permute-done.11.refs_0_, bf16[512,1024]{1,0:T(8,128)(2,1)S(1)} %collective-permute-done.12.refs_1_, bf16[4096,384]{1,0:T(8,128)(2,1)} %bitcast.41, ...), custom_call_target="tpu_custom_call" | custom-call | flops 2415919104 | bytes 13631488 | tf_op jit(solution)/shard_map/pallas_call | solution.py:324
  161.7 3.3 %collective-permute-start.18 = (bf16[256,1024]{1,0:T(8,128)(2,1)S(1)}, bf16[256,1024]{1,0:T(8,128)(2,1)S(1)}, u32[]{:S(2)}, u32[]{:S(2)}) collective-permute-start(bf16[256,1024]{1,0:T(8,128)(2,1)S(1)} %slice.45), channel_id=1, source_target_pairs={{0,64},{64,128},{128,192},{192,0},{1,65},{65,129},{129,193},{193,1... | collective-permute-start | bytes 1572872 | tf_op jit(solution)/shard_map/ppermute | solution.py:43
  165.0 1.0 collective-permute-done.13.refs_0_
  165.9 5.9 %shard_map.182 = (bf16[256,1024]{1,0:T(8,128)(2,1)S(1)}, bf16[256,1024]{1,0:T(8,128)(2,1)S(1)}) custom-call(bf16[256,256]{1,0:T(8,128)(2,1)S(1)} %copy-done.3, bf16[256,1024]{1,0:T(8,128)(2,1)S(1)} %collective-permute-done.13.refs_0_, bf16[256,1024]{1,0:T(8,128)(2,1)S(1)} %collective-permute-done.14.refs_1_, bf16[4096,384]{1,0:T(8,128)(2,1)S(1)} %bitcast.43, ...), custom_call_target="tpu_custom_call" | custom-call | flops 1207959552 | bytes 11534336 | tf_op jit(solution)/shard_map/pallas_call | solution.py:324
  171.8 2.4 collective-permute-start.15
  174.2 2.1 collective-permute-done.18
  176.3 3.4 %collective-permute-done.17 = bf16[256,1024]{1,0:T(8,128)(2,1)S(1)} collective-permute-done((bf16[256,1024]{1,0:T(8,128)(2,1)S(1)}, bf16[256,1024]{1,0:T(8,128)(2,1)S(1)}, u32[]{:S(2)}, u32[]{:S(2)}) %collective-permute-start.17) | collective-permute-done | bytes 524320 | tf_op jit(solution)/shard_map/ppermute | solution.py:43
  179.7 0.4 convert_add_fusion
  180.1 4.9 %collective-permute-done.15 = bf16[256,1024]{1,0:T(8,128)(2,1)S(1)} collective-permute-done((bf16[256,1024]{1,0:T(8,128)(2,1)S(1)}, bf16[256,1024]{1,0:T(8,128)(2,1)S(1)}, u32[]{:S(2)}, u32[]{:S(2)}) %collective-permute-start.15) | collective-permute-done | bytes 524320 | tf_op jit(solution)/shard_map/ppermute | solution.py:43
  185.0 3.4 %collective-permute-done.16 = bf16[256,1024]{1,0:T(8,128)(2,1)S(1)} collective-permute-done((bf16[256,1024]{1,0:T(8,128)(2,1)S(1)}, bf16[256,1024]{1,0:T(8,128)(2,1)S(1)}, u32[]{:S(2)}, u32[]{:S(2)}) %collective-permute-start.16) | collective-permute-done | bytes 524320 | tf_op jit(solution)/shard_map/ppermute | solution.py:43
  188.4 0.2 add_convert_fusion.3
  188.6 0.4 collective-permute-start.19
  189.0 0.2 add_convert_fusion.1
  189.2 2.1 collective-permute-start.20
  191.3 8.8 %collective-permute-done.19 = bf16[256,1024]{1,0:T(8,128)(2,1)S(1)} collective-permute-done((bf16[256,1024]{1,0:T(8,128)(2,1)S(1)}, bf16[256,1024]{1,0:T(8,128)(2,1)S(1)}, u32[]{:S(2)}, u32[]{:S(2)}) %collective-permute-start.19) | collective-permute-done | bytes 524320 | tf_op jit(solution)/shard_map/ppermute | solution.py:43
  200.1 0.1 add_convert_fusion.2
  200.3 1.6 collective-permute-done.20
  201.9 0.1 add_convert_fusion
  202.0 1.0 maximum_bitcast_fusion
  203.1 7.7 %all-to-all-start.3 = ((bf16[64,8,1024]{2,1,0:T(8,128)(2,1)}), bf16[64,8,1024]{2,1,0:T(8,128)(2,1)S(1)}, u32[]{:S(2)}, u32[]{:S(2)}) async-start(bf16[64,8,1024]{2,1,0:T(8,128)(2,1)} %maximum_bitcast_fusion), calls=%async_computation.3 | async-start | bytes 2097152 | tf_op jit(solution)/shard_map/all_to_all | solution.py:423
  211.4 0.4 and_select_fusion
  211.8 0.5 select_n.151
  212.4 27.2 %all-to-all-done.3 = bf16[64,8,1024]{2,1,0:T(8,128)(2,1)S(1)} async-done(((bf16[64,8,1024]{2,1,0:T(8,128)(2,1)}), bf16[64,8,1024]{2,1,0:T(8,128)(2,1)S(1)}, u32[]{:S(2)}, u32[]{:S(2)}) %all-to-all-start.3) | async-done | bytes 1048608 | tf_op jit(solution)/shard_map/all_to_all | solution.py:423
  239.6 0.9 shard_map.183
  (74 shorter events, 2.2 us)
Async XLA Ops:
  1.9 24.6 %copy-start.13 = (s32[8]{0:T(128)S(1)}, s32[8]{0:T(128)}, u32[]{:S(2)}) copy-start(s32[8]{0:T(128)} %param.24) | copy-start | bytes 100
  1.9 24.6 %copy-start.14 = (s32[8]{0:T(128)S(1)}, s32[8]{0:T(128)}, u32[]{:S(2)}) copy-start(s32[8]{0:T(128)} %param.25) | copy-start | bytes 100
  2.0 25.4 %copy-start.9 = (bf16[8,8192]{1,0:T(8,128)(2,1)S(1)}, bf16[8,8192]{1,0:T(8,128)(2,1)}, u32[]{:S(2)}) copy-start(bf16[8,8192]{1,0:T(8,128)(2,1)} %param.18) | copy-start | bytes 393220
  2.0 17.3 %collective-permute-start.4 = (bf16[128,2048]{1,0:T(8,128)(2,1)S(1)}, bf16[128,2048]{1,0:T(8,128)(2,1)S(1)}, u32[]{:S(2)}, u32[]{:S(2)}) collective-permute-start(bf16[128,2048]{1,0:T(8,128)(2,1)S(1)} %get-tuple-element.67), channel_id=1, source_target_pairs={{0,1},{1,0},{2,3},{3,2},{4,5},{5,4},{6,7},{7,6},{8,9},{9,8},{10,11... | collective-permute-start | bytes 1572872 | tf_op jit(solution)/shard_map/ppermute | solution.py:51
  4.7 4.8 %collective-permute-start.2 = (s32[4]{0:T(128)S(1)}, s32[4]{0:T(128)S(1)}, u32[]{:S(2)}, u32[]{:S(2)}) collective-permute-start(s32[4]{0:T(128)S(1)} %get-tuple-element.72), channel_id=1, source_target_pairs={{0,192},{64,0},{128,64},{192,128},{1,193},{65,1},{129,65},{193,129... | collective-permute-start | bytes 56 | tf_op jit(solution)/shard_map/ppermute | solution.py:43
  5.5 5.0 %collective-permute-start.1 = (s32[4]{0:T(128)S(1)}, s32[4]{0:T(128)S(1)}, u32[]{:S(2)}, u32[]{:S(2)}) collective-permute-start(s32[4]{0:T(128)S(1)} %get-tuple-element.73), channel_id=1, source_target_pairs={{0,128},{64,192},{128,0},{192,64},{1,129},{65,193},{129,1},{193,65... | collective-permute-start | bytes 56 | tf_op jit(solution)/shard_map/ppermute | solution.py:43
  8.2 3.5 %collective-permute-start = (s32[4]{0:T(128)S(1)}, s32[4]{0:T(128)S(1)}, u32[]{:S(2)}, u32[]{:S(2)}) collective-permute-start(s32[4]{0:T(128)S(1)} %get-tuple-element.74), channel_id=1, source_target_pairs={{0,64},{64,128},{128,192},{192,0},{1,65},{65,129},{129,193},{193,1... | collective-permute-start | bytes 56 | tf_op jit(solution)/shard_map/ppermute | solution.py:43
  15.0 8.5 %collective-permute-start.3 = (bf16[4,2,16,512]{3,2,1,0:T(8,128)(2,1)}, bf16[4,2,16,512]{3,2,1,0:T(8,128)(2,1)S(1)}, u32[]{:S(2)}, u32[]{:S(2)}) collective-permute-start(bf16[4,2,16,512]{3,2,1,0:T(8,128)(2,1)} %get-tuple-element.31), channel_id=1, source_target_pairs={{0,192},{64,0},{128,64},{192,128},{1,193},{65,1},{129,65},{193,129... | collective-permute-start | bytes 393224 | tf_op jit(solution)/shard_map/ppermute | solution.py:43
  15.8 12.2 %collective-permute-start.5 = (bf16[4,2,16,512]{3,2,1,0:T(8,128)(2,1)}, bf16[4,2,16,512]{3,2,1,0:T(8,128)(2,1)S(1)}, u32[]{:S(2)}, u32[]{:S(2)}) collective-permute-start(bf16[4,2,16,512]{3,2,1,0:T(8,128)(2,1)} %get-tuple-element.33), channel_id=1, source_target_pairs={{0,128},{64,192},{128,0},{192,64},{1,129},{65,193},{129,1},{193,65... | collective-permute-start | bytes 393224 | tf_op jit(solution)/shard_map/ppermute | solution.py:43
  18.2 9.8 %collective-permute-start.6 = (bf16[4,2,16,512]{3,2,1,0:T(8,128)(2,1)}, bf16[4,2,16,512]{3,2,1,0:T(8,128)(2,1)S(1)}, u32[]{:S(2)}, u32[]{:S(2)}) collective-permute-start(bf16[4,2,16,512]{3,2,1,0:T(8,128)(2,1)} %get-tuple-element.34), channel_id=1, source_target_pairs={{0,64},{64,128},{128,192},{192,0},{1,65},{65,129},{129,193},{193,1... | collective-permute-start | bytes 393224 | tf_op jit(solution)/shard_map/ppermute | solution.py:43
  23.5 4.5 %copy-start.6 = (bf16[4,2,16,512]{3,2,1,0:T(8,128)(2,1)}, bf16[4,2,16,512]{3,2,1,0:T(8,128)(2,1)S(1)}, u32[]{:S(2)}) copy-start(bf16[4,2,16,512]{3,2,1,0:T(8,128)(2,1)S(1)} %collective-permute-done.3.b1) | copy-start | bytes 393220
  23.6 10.7 %collective-permute-start.9 = (bf16[256,512]{1,0:T(8,128)(2,1)S(1)}, bf16[256,512]{1,0:T(8,128)(2,1)S(1)}, u32[]{:S(2)}, u32[]{:S(2)}) collective-permute-start(bf16[256,512]{1,0:T(8,128)(2,1)S(1)} %get-tuple-element.62), channel_id=1, source_target_pairs={{0,6},{1,7},{2,0},{3,1},{4,2},{5,3},{6,4},{7,5},{8,14},{9,15},{10,... | collective-permute-start | bytes 786440 | tf_op jit(solution)/shard_map/ppermute | solution.py:51
  24.7 9.6 %collective-permute-start.8 = (bf16[256,512]{1,0:T(8,128)(2,1)S(1)}, bf16[256,512]{1,0:T(8,128)(2,1)S(1)}, u32[]{:S(2)}, u32[]{:S(2)}) collective-permute-start(bf16[256,512]{1,0:T(8,128)(2,1)S(1)} %get-tuple-element.63), channel_id=1, source_target_pairs={{0,4},{1,5},{2,6},{3,7},{4,0},{5,1},{6,2},{7,3},{8,12},{9,13},{10,... | collective-permute-start | bytes 786440 | tf_op jit(solution)/shard_map/ppermute | solution.py:51
  25.6 10.7 %collective-permute-start.7 = (bf16[256,512]{1,0:T(8,128)(2,1)S(1)}, bf16[256,512]{1,0:T(8,128)(2,1)S(1)}, u32[]{:S(2)}, u32[]{:S(2)}) collective-permute-start(bf16[256,512]{1,0:T(8,128)(2,1)S(1)} %get-tuple-element.64), channel_id=1, source_target_pairs={{0,2},{1,3},{2,4},{3,5},{4,6},{5,7},{6,0},{7,1},{8,10},{9,11},{10,... | collective-permute-start | bytes 786440 | tf_op jit(solution)/shard_map/ppermute | solution.py:51
  28.0 0.7 copy-start.7
  28.0 0.7 copy-start.8
  28.7 42.5 %copy-start.10 = (s32[8,8]{1,0:T(8,128)S(1)}, s32[8,8]{1,0:T(8,128)}, u32[]{:S(2)}) copy-start(s32[8,8]{1,0:T(8,128)} %param.28) | copy-start | bytes 772
  28.7 42.7 %copy-start.12 = (bf16[4096]{0:T(1024)(128)(2,1)S(1)}, bf16[4096]{0:T(1024)(128)(2,1)}, u32[]{:S(2)}) copy-start(bf16[4096]{0:T(1024)(128)(2,1)} %param.27) | copy-start | bytes 24580
  34.3 54.1 %copy-start.4 = (bf16[8,4096]{1,0:T(8,128)(2,1)S(1)}, bf16[8,4096]{1,0:T(8,128)(2,1)}, u32[]{:S(2)}) copy-start(bf16[8,4096]{1,0:T(8,128)(2,1)} %residual_ref.1) | copy-start | bytes 196612
  61.2 1.9 collective-permute-start.10
  64.4 0.8 copy-start.2
  65.2 62.7 %copy-start = (bf16[1,4096,384]{2,1,0:T(8,128)(2,1)S(1)}, bf16[1,4096,384]{2,1,0:T(8,128)(2,1)}, u32[]{:S(2)}) copy-start(bf16[1,4096,384]{2,1,0:T(8,128)(2,1)} %param.30) | copy-start | bytes 9437188
  65.2 62.7 %copy-start.3 = (bf16[256,256]{1,0:T(8,128)(2,1)S(1)}, bf16[256,256]{1,0:T(8,128)(2,1)}, u32[]{:S(2)}) copy-start(bf16[256,256]{1,0:T(8,128)(2,1)} %constant.113.clone.order_ref) | copy-start | bytes 393220
  65.2 23.3 %all-to-all-start.1 = ((bf16[64,8,512]{2,1,0:T(8,128)(2,1)}), bf16[64,8,512]{2,1,0:T(8,128)(2,1)}, u32[]{:S(2)}, u32[]{:S(2)}) async-start(bf16[64,8,512]{2,1,0:T(8,128)(2,1)} %bitcast.48), calls=%async_computation.1 | async-start | bytes 1048576 | tf_op jit(solution)/shard_map/all_to_all | solution.py:239
  124.7 25.4 %collective-permute-start.12 = (bf16[512,1024]{1,0:T(8,128)(2,1)S(1)}, bf16[512,1024]{1,0:T(8,128)(2,1)S(1)}, u32[]{:S(2)}, u32[]{:S(2)}) collective-permute-start(bf16[512,1024]{1,0:T(8,128)(2,1)S(1)} %bitcast.44), channel_id=1, source_target_pairs={{0,192},{64,0},{128,64},{192,128},{1,193},{65,1},{129,65},{193,129... | collective-permute-start | bytes 3145736 | tf_op jit(solution)/shard_map/ppermute | solution.py:43
  124.8 25.4 %collective-permute-start.11 = (bf16[512,1024]{1,0:T(8,128)(2,1)S(1)}, bf16[512,1024]{1,0:T(8,128)(2,1)S(1)}, u32[]{:S(2)}, u32[]{:S(2)}) collective-permute-start(bf16[512,1024]{1,0:T(8,128)(2,1)S(1)} %bitcast.45), channel_id=1, source_target_pairs={{0,64},{64,128},{128,192},{192,0},{1,65},{65,129},{129,193},{193,1... | collective-permute-start | bytes 3145736 | tf_op jit(solution)/shard_map/ppermute | solution.py:43
  150.2 14.8 %collective-permute-start.14 = (bf16[256,1024]{1,0:T(8,128)(2,1)S(1)}, bf16[256,1024]{1,0:T(8,128)(2,1)S(1)}, u32[]{:S(2)}, u32[]{:S(2)}) collective-permute-start(bf16[256,1024]{1,0:T(8,128)(2,1)S(1)} %slice.41), channel_id=1, source_target_pairs={{0,64},{64,128},{128,192},{192,0},{1,65},{65,129},{129,193},{193,1... | collective-permute-start | bytes 1572872 | tf_op jit(solution)/shard_map/ppermute | solution.py:43
  153.2 12.7 %collective-permute-start.13 = (bf16[256,1024]{1,0:T(8,128)(2,1)S(1)}, bf16[256,1024]{1,0:T(8,128)(2,1)S(1)}, u32[]{:S(2)}, u32[]{:S(2)}) collective-permute-start(bf16[256,1024]{1,0:T(8,128)(2,1)S(1)} %slice.40), channel_id=1, source_target_pairs={{0,192},{64,0},{128,64},{192,128},{1,193},{65,1},{129,65},{193,129... | collective-permute-start | bytes 1572872 | tf_op jit(solution)/shard_map/ppermute | solution.py:43
  153.2 12.7 %copy-start.1 = (bf16[1,4096,384]{2,1,0:T(8,128)(2,1)S(1)}, bf16[1,4096,384]{2,1,0:T(8,128)(2,1)}, u32[]{:S(2)}) copy-start(bf16[1,4096,384]{2,1,0:T(8,128)(2,1)} %param.30) | copy-start | bytes 9437188
  161.7 14.6 %collective-permute-start.18 = (bf16[256,1024]{1,0:T(8,128)(2,1)S(1)}, bf16[256,1024]{1,0:T(8,128)(2,1)S(1)}, u32[]{:S(2)}, u32[]{:S(2)}) collective-permute-start(bf16[256,1024]{1,0:T(8,128)(2,1)S(1)} %slice.45), channel_id=1, source_target_pairs={{0,64},{64,128},{128,192},{192,0},{1,65},{65,129},{129,193},{193,1... | collective-permute-start | bytes 1572872 | tf_op jit(solution)/shard_map/ppermute | solution.py:43
  165.0 14.7 %collective-permute-start.17 = (bf16[256,1024]{1,0:T(8,128)(2,1)S(1)}, bf16[256,1024]{1,0:T(8,128)(2,1)S(1)}, u32[]{:S(2)}, u32[]{:S(2)}) collective-permute-start(bf16[256,1024]{1,0:T(8,128)(2,1)S(1)} %slice.43), channel_id=1, source_target_pairs={{0,192},{64,0},{128,64},{192,128},{1,193},{65,1},{129,65},{193,129... | collective-permute-start | bytes 1572872 | tf_op jit(solution)/shard_map/ppermute | solution.py:43
  171.8 13.2 %collective-permute-start.15 = (bf16[256,1024]{1,0:T(8,128)(2,1)S(1)}, bf16[256,1024]{1,0:T(8,128)(2,1)S(1)}, u32[]{:S(2)}, u32[]{:S(2)}) collective-permute-start(bf16[256,1024]{1,0:T(8,128)(2,1)S(1)} %get-tuple-element.49), channel_id=1, source_target_pairs={{0,64},{64,128},{128,192},{192,0},{1,65},{65,129},{129,193},{193,1... | collective-permute-start | bytes 1572872 | tf_op jit(solution)/shard_map/ppermute | solution.py:43
  174.2 14.2 %collective-permute-start.16 = (bf16[256,1024]{1,0:T(8,128)(2,1)S(1)}, bf16[256,1024]{1,0:T(8,128)(2,1)S(1)}, u32[]{:S(2)}, u32[]{:S(2)}) collective-permute-start(bf16[256,1024]{1,0:T(8,128)(2,1)S(1)} %get-tuple-element.50), channel_id=1, source_target_pairs={{0,192},{64,0},{128,64},{192,128},{1,193},{65,1},{129,65},{193,129... | collective-permute-start | bytes 1572872 | tf_op jit(solution)/shard_map/ppermute | solution.py:43
  188.6 11.5 %collective-permute-start.19 = (bf16[256,1024]{1,0:T(8,128)(2,1)S(1)}, bf16[256,1024]{1,0:T(8,128)(2,1)S(1)}, u32[]{:S(2)}, u32[]{:S(2)}) collective-permute-start(bf16[256,1024]{1,0:T(8,128)(2,1)S(1)} %add_convert_fusion.3), channel_id=1, source_target_pairs={{0,64},{64,128},{128,192},{192,0},{1,65},{65,129},{129,193},{193,1... | collective-permute-start | bytes 1572872 | tf_op jit(solution)/shard_map/ppermute | solution.py:43
  189.2 12.7 %collective-permute-start.20 = (bf16[256,1024]{1,0:T(8,128)(2,1)S(1)}, bf16[256,1024]{1,0:T(8,128)(2,1)S(1)}, u32[]{:S(2)}, u32[]{:S(2)}) collective-permute-start(bf16[256,1024]{1,0:T(8,128)(2,1)S(1)} %add_convert_fusion.1), channel_id=1, source_target_pairs={{0,192},{64,0},{128,64},{192,128},{1,193},{65,1},{129,65},{193,129... | collective-permute-start | bytes 1572872 | tf_op jit(solution)/shard_map/ppermute | solution.py:43
  200.2 10.7 %copy-start.11 = (f32[8,8]{1,0:T(8,128)S(1)}, f32[8,8]{1,0:T(8,128)}, u32[]{:S(2)}) copy-start(f32[8,8]{1,0:T(8,128)} %param.29) | copy-start | bytes 772
  203.1 36.6 %copy-start.5 = (bf16[8,4096]{1,0:T(8,128)(2,1)S(1)}, bf16[8,4096]{1,0:T(8,128)(2,1)}, u32[]{:S(2)}) copy-start(bf16[8,4096]{1,0:T(8,128)(2,1)} %get-tuple-element.28.attended_ref) | copy-start | bytes 196612
  203.1 36.6 %all-to-all-start.3 = ((bf16[64,8,1024]{2,1,0:T(8,128)(2,1)}), bf16[64,8,1024]{2,1,0:T(8,128)(2,1)S(1)}, u32[]{:S(2)}, u32[]{:S(2)}) async-start(bf16[64,8,1024]{2,1,0:T(8,128)(2,1)} %maximum_bitcast_fusion), calls=%async_computation.3 | async-start | bytes 2097152 | tf_op jit(solution)/shard_map/all_to_all | solution.py:423
